TPU v7x, 32 devices: a whole 2x2x4 slice. The times are simulated.
32 devices in a mesh: group: 2 (over x), node: 16 (over z, y, core).
Axes of the slice: x: 2, y: 2, z: 4, core: 2. Of those that a mesh axis runs over, the one named last changes fastest.
Arguments:
- tokens: bfloat16 [2048, 3584], P(('group', 'node')), parts along dimension 0, may hold values from -6 to 6
- expert_ids: int32 [2048, 8], P(('group', 'node')), parts along dimension 0, may hold values from 0 to 15, all different within a row; in each aligned block of 64 rows (0 to 63, 64 to 127, ...) at most 40 rows name the same one
- gate_scores: float32 [2048, 8], P(('group', 'node')), parts along dimension 0, may hold values from 0.05 to 1
- w_gate: bfloat16 [3584, 16384], P(None, 'node'), may hold values from -0.09375 to 0.09375
- w_up: bfloat16 [3584, 16384], P(None, 'node'), may hold values from -0.09375 to 0.09375
- w_down: bfloat16 [16384, 3584], P('node'), may hold values from -0.1875 to 0.1875
Outputs:
- combined: bfloat16 [2048, 3584], P(('group', 'node')), parts along dimension 0
There are 2 independent parts, one for each index of `group`. A program takes and returns all parts, laid end to end along the dimension named above; an argument that names none is the same for every part. Nothing has to cross between parts.
Inputs may be any that keep to these rules, and one draw needn't show every extreme that they name: `expert_ids`: each row names 8 different experts. In the 64 rows of one device no expert is named by more than 40 rows, a bound that some block reaches.
All inputs are finite; a program needn't handle non-finite values.
Results may differ from a plain program's by a relative error of at most 0.0058.
Values may be sent and summed in bfloat16 or wider, within the bound.
A program may use at most 128 MiB of HBM per device.

v0:
```python
import jax
import jax.numpy as jnp
from jax import lax
from jax.sharding import PartitionSpec as P

ROUTE_SCALE = 2.5


def shards(tokens, expert_ids, gate_scores, w_gate, w_up, w_down):
    node_count = lax.axis_size("node")
    row_count, features = tokens.shape
    top = expert_ids.shape[1]
    experts = max(16, node_count // 2)
    slices = node_count // experts
    capacity = 5 * row_count * top // (4 * experts)
    weights = ROUTE_SCALE * gate_scores / jnp.sum(gate_scores, axis=1, keepdims=True)
    flat_ids = expert_ids.reshape(-1)
    marks = (flat_ids[:, None] == jnp.arange(experts, dtype=jnp.int32)[None, :]).astype(jnp.int32)
    ranks = jnp.sum(jnp.cumsum(marks, axis=0) * marks, axis=1) - 1
    slot_of = (flat_ids * capacity + ranks).reshape(row_count, top)
    columns = jnp.arange(experts * capacity, dtype=jnp.int32)
    hits = slot_of[:, :, None] == columns[None, None, :]
    dispatch = jnp.any(hits, axis=1).astype(jnp.bfloat16)
    combine_table = jnp.sum(jnp.where(hits, weights[:, :, None], 0.0), axis=1)
    packed = jnp.dot(jnp.transpose(dispatch), tokens, preferred_element_type=jnp.float32).astype(
        jnp.bfloat16
    )
    packed = packed.reshape(experts, capacity, features)
    send_rows = jnp.repeat(packed, slices, axis=0)
    received = lax.all_to_all(send_rows, "node", split_axis=0, concat_axis=0, tiled=True)
    slot_count = received.shape[1]
    flat_rows = received.reshape(node_count * slot_count, features)
    gate_part = jnp.dot(flat_rows, w_gate, preferred_element_type=jnp.float32)
    up_part = jnp.dot(flat_rows, w_up, preferred_element_type=jnp.float32)
    hidden = (jax.nn.silu(gate_part) * up_part).astype(jnp.bfloat16)
    piece = jnp.dot(hidden, w_down, preferred_element_type=jnp.float32).astype(jnp.bfloat16)
    piece = piece.reshape(node_count, slot_count, features)
    returned = lax.all_to_all(piece, "node", split_axis=0, concat_axis=0, tiled=True)
    summed = jnp.sum(
        returned.astype(jnp.float32).reshape(experts, slices, slot_count, features), axis=1
    )
    rounded = lax.optimization_barrier(summed.astype(jnp.bfloat16))
    expert_outputs = rounded.astype(jnp.float32)
    combined = jnp.dot(
        combine_table,
        expert_outputs.reshape(experts * capacity, features),
        precision=lax.Precision.HIGHEST,
        preferred_element_type=jnp.float32,
    )
    return combined.astype(jnp.bfloat16)


def solution(mesh):
    return jax.shard_map(
        shards,
        mesh=mesh,
        in_specs=(
            P(("group", "node"), None),
            P(("group", "node"), None),
            P(("group", "node"), None),
            P(None, "node"),
            P(None, "node"),
            P("node", None),
        ),
        out_specs=P(("group", "node"), None),
        check_vma=False,
    )
```

profile of v0, /device:TPU:16, one launch (start us, length us, event | category | flops | bytes accessed | tf_op | source)
XLA Modules:
  0.0 248.7 jit_solution(10385130764461320458)
XLA Ops:
  0.0 0.0 copy-start
  0.0 0.8 copy.21
  0.8 0.1 eq.42
  0.9 0.1 eq.38
  1.0 1.2 reduce-window.6
  2.2 0.2 slice_reduce_fusion
  2.4 0.1 fusion.2
  2.5 0.1 sub.7
  2.6 0.1 copy.24
  2.7 0.7 multiply_add_fusion
  3.4 0.1 copy.25
  3.5 0.5 fusion
  4.0 0.0 copy-done
  4.0 0.0 slice-start
  4.0 1.4 convolution_convert_fusion
  5.4 0.0 slice-start.1
  5.4 107.3 %all_to_all.10 = bf16[16,40,3584]{2,1,0:T(8,128)(2,1)S(1)} all-to-all(bf16[16,40,3584]{2,1,0:T(8,128)(2,1)S(1)} %bitcast.37), channel_id=1, replica_groups=mesh['group'=2,'node'=16] {'node'}, dimensions={0} | all-to-all | bytes 9175040 | tf_op jit(solution)/shard_map/all_to_all | solution.py:30
  112.7 0.0 copy-start.1
  112.7 2.1 copy-done.1
  114.9 0.0 slice-done
  114.9 0.0 slice-done.1
  114.9 4.9 %fusion.4 = f32[640,1024]{1,0:T(8,128)S(1)} fusion(bf16[640,3584]{1,0:T(8,128)(2,1)S(1)} %bitcast.39, bf16[3584,1024]{1,0:T(8,128)(2,1)S(1)} %bitcast.42), kind=kOutput, calls=%fused_computation.18 | convolution fusion | flops 4697620480 | bytes 14548992 | tf_op jit(solution)/shard_map/dot_general | solution.py:33
  119.8 17.2 %convolution_convert_fusion.1 = bf16[640,3584]{1,0:T(8,128)(2,1)} fusion(bf16[1024,3584]{1,0:T(8,128)(2,1)} %param.11, f32[640,1024]{1,0:T(8,128)S(1)} %fusion.4, bf16[640,3584]{1,0:T(8,128)(2,1)} %bitcast.40, bf16[3584,1024]{1,0:T(8,128)(2,1)} %param.10), kind=kOutput, calls=%fused_computation.1 | convolution fusion | flops 9401466880 | bytes 26476544 | tf_op jit(solution)/shard_map/dot_general | solution.py:36
  136.9 0.0 copy-start.2
  136.9 5.1 %all-to-all-start.1 = ((bf16[16,40,3584]{2,1,0:T(8,128)(2,1)}), bf16[16,40,3584]{2,1,0:T(8,128)(2,1)}, u32[]{:S(2)}, u32[]{:S(2)}) async-start(bf16[16,40,3584]{2,1,0:T(8,128)(2,1)} %bitcast.38), calls=%async_computation.1 | async-start | bytes 9175040 | tf_op jit(solution)/shard_map/all_to_all | solution.py:38
  142.0 0.0 copy-done.2
  142.1 0.1 copy.26
  142.2 0.5 select_reduce_fusion
  142.6 100.5 %all-to-all-done.1 = bf16[16,40,3584]{2,1,0:T(8,128)(2,1)} async-done(((bf16[16,40,3584]{2,1,0:T(8,128)(2,1)}), bf16[16,40,3584]{2,1,0:T(8,128)(2,1)}, u32[]{:S(2)}, u32[]{:S(2)}) %all-to-all-start.1) | async-done | bytes 4587552 | tf_op jit(solution)/shard_map/all_to_all | solution.py:38
  243.2 5.5 %convolution_convert_fusion.2 = bf16[64,3584]{1,0:T(8,128)(2,1)} fusion(f32[64,640]{1,0:T(8,128)S(1)} %select_reduce_fusion, bf16[640,3584]{1,0:T(8,128)(2,1)} %bitcast.4), kind=kOutput, calls=%fused_computation.2 | convolution fusion | flops 1761837056 | bytes 5210112 | tf_op jit(solution)/shard_map/dot_general | solution.py:44
  (7 shorter events, 0.1 us)
Async XLA Ops:
  0.0 4.0 %copy-start = (bf16[64,3584]{1,0:T(8,128)(2,1)S(1)}, bf16[64,3584]{1,0:T(8,128)(2,1)}, u32[]{:S(2)}) copy-start(bf16[64,3584]{1,0:T(8,128)(2,1)} %param.6) | copy-start | bytes 1376260
  4.0 110.9 %slice-start = ((s8[7340032]{0:T(1024)(128)(4,1)}), s8[4194304]{0:T(1024)(128)(4,1)S(1)}, s32[]{:S(2)}) async-start(s8[7340032]{0:T(1024)(128)(4,1)} %bitcast.41), calls=%async_computation.2 | async-start | bytes 8388608
  5.4 109.5 %slice-start.1 = ((s8[7340032]{0:T(1024)(128)(4,1)}), s8[3145728]{0:T(1024)(128)(4,1)S(1)}, s32[]{:S(2)}) async-start(s8[7340032]{0:T(1024)(128)(4,1)} %bitcast.41), calls=%async_computation.3 | async-start | bytes 6291456
  112.7 2.1 copy-start.1
  136.9 5.1 %copy-start.2 = (f32[64,8]{0,1:T(8,128)S(1)}, f32[64,8]{0,1:T(8,128)}, u32[]{:S(2)}) copy-start(f32[64,8]{0,1:T(8,128)} %param.8) | copy-start | bytes 6148
  136.9 106.2 %all-to-all-start.1 = ((bf16[16,40,3584]{2,1,0:T(8,128)(2,1)}), bf16[16,40,3584]{2,1,0:T(8,128)(2,1)}, u32[]{:S(2)}, u32[]{:S(2)}) async-start(bf16[16,40,3584]{2,1,0:T(8,128)(2,1)} %bitcast.38), calls=%async_computation.1 | async-start | bytes 9175040 | tf_op jit(solution)/shard_map/all_to_all | solution.py:38
where the time goes:
time: 249 us
  blocking collectives  107 us (43%)
  waiting for transfers between devices  101 us (41%)
  matrix products  29 us (12%)
  starting transfers between devices  5.1 us (2%)
  local copies, waits for them, and re-layouts  3.72 us (1%)
  other arithmetic  2.95 us (1%)
    all_to_all x1, blocking collectives, shards(): lax.all_to_all(send_rows, 'node', split_axis=0, concat_axis=0, tiled=True)  107 us
    all_to_all x1, waiting for transfers between devices, shards(): lax.all_to_all(piece, 'node', split_axis=0, concat_axis=0, tiled=True)  101 us
    dot_general x1, matrix products, shards(): jnp.dot(hidden, w_down, preferred_element_type=jnp.float32)  17.2 us
    dot_general x1, matrix products, shards(): jnp.dot(combine_table, expert_outputs.reshape(experts * capacity, feature...  5.54 us
    all_to_all x1, starting transfers between devices, shards(): lax.all_to_all(piece, 'node', split_axis=0, concat_axis=0, tiled=True)  5.1 us
  transfers between devices with their start and end apart: 1, of which 1 were waited for; matrix products, arithmetic and copies ran while one was open for 0% of the time, Pallas kernels for 0%

commit v1 on v0

v1 whole, which is shorter than its diff:
```python
import jax
import jax.numpy as jnp
from jax import lax
from jax.sharding import PartitionSpec as P

ROUTE_SCALE = 2.5


def shards(tokens, expert_ids, gate_scores, w_gate, w_up, w_down):
    node_count = lax.axis_size("node")
    experts = max(16, node_count // 2)
    slices = node_count // experts
    weights = ROUTE_SCALE * gate_scores / jnp.sum(gate_scores, axis=1, keepdims=True)
    marks = expert_ids[:, :, None] == jnp.arange(experts, dtype=jnp.int32)[None, None, :]
    table = jnp.sum(jnp.where(marks, weights[:, :, None], 0.0), axis=1)
    all_table = lax.all_gather(table, "node", axis=0, tiled=True)
    own = lax.axis_index("node") // slices
    share = lax.dynamic_slice_in_dim(all_table, own, 1, 1)
    rows = lax.all_gather(tokens, "node", axis=0, tiled=True)
    gate_part = jnp.dot(rows, w_gate, preferred_element_type=jnp.float32)
    up_part = jnp.dot(rows, w_up, preferred_element_type=jnp.float32)
    hidden = (jax.nn.silu(gate_part) * up_part).astype(jnp.bfloat16)
    piece = jnp.dot(hidden, w_down, preferred_element_type=jnp.float32)
    part = (piece * share).astype(jnp.bfloat16)
    return lax.psum_scatter(part, "node", scatter_dimension=0, tiled=True)


def solution(mesh):
    return jax.shard_map(
        shards,
        mesh=mesh,
        in_specs=(
            P(("group", "node"), None),
            P(("group", "node"), None),
            P(("group", "node"), None),
            P(None, "node"),
            P(None, "node"),
            P("node", None),
        ),
        out_specs=P(("group", "node"), None),
        check_vma=False,
    )
```

time: 249 us -> 216 us (0.87)
  blocking collectives: 107 us -> 16.6 us
  waiting for transfers between devices: 101 us -> 144 us
  between operations: 0.1 us -> 13.4 us
  matrix products: 29 us -> 37.9 us
  starting transfers between devices: 5.1 us -> 0.04 us
  local copies, waits for them, and re-layouts: 3.72 us -> 0.15 us
    all_to_all x1 -> x0, blocking collectives: 107 us -> none  [shards(): lax.all_to_all(send_rows, 'node', split_axis=0, concat_axis=0, tiled=True)]
    all_to_all x1 -> x0, waiting for transfers between devices: 101 us -> none  [shards(): lax.all_to_all(piece, 'node', split_axis=0, concat_axis=0, tiled=True)]
    reduce_scatter x0 -> x1, waiting for transfers between devices: none -> 90.5 us  [shards(): return lax.psum_scatter(part, 'node', scatter_dimension=0, tiled=True)]
    all_gather x0 -> x1, waiting for transfers between devices: none -> 52.4 us  [shards(): rows = lax.all_gather(tokens, 'node', axis=0, tiled=True)]
    all_gather x0 -> x1, blocking collectives: none -> 16.6 us  [shards(): all_table = lax.all_gather(table, 'node', axis=0, tiled=True)]
    dot_general x4 -> x2, matrix products: 29 us -> 37.9 us  [the longest x1 24.4 us: shards(): piece = jnp.dot(hidden, w_down, preferred_element_type=jnp.float32)]
    all_to_all x1 -> x0, starting transfers between devices: 5.1 us -> none  [shards(): lax.all_to_all(piece, 'node', split_axis=0, concat_axis=0, tiled=True)]
    unnamed x11 -> x1, local copies, waits for them, and re-layouts: 2.99 us -> 0.1 us
  transfers between devices with their start and end apart: 1 -> 2, of which waited for: 1 -> 2; matrix products, arithmetic and copies ran while one was open for 0% -> 1% of each run, Pallas kernels for 0% -> 0%
where the time goes in v1:
time: 216 us; the launch traced here: 214 us
  waiting for transfers between devices  144 us (67%)
  matrix products  37.9 us (18%)
  blocking collectives  16.6 us (8%)
  between operations  13.4 us (6%)
    reduce_scatter x1, waiting for transfers between devices, shards(): return lax.psum_scatter(part, 'node', scatter_dimension=0, tiled=True)  90.5 us
    all_gather x1, waiting for transfers between devices, shards(): rows = lax.all_gather(tokens, 'node', axis=0, tiled=True)  52.4 us
    dot_general x1, matrix products, shards(): piece = jnp.dot(hidden, w_down, preferred_element_type=jnp.float32)  24.4 us
    all_gather x1, blocking collectives, shards(): all_table = lax.all_gather(table, 'node', axis=0, tiled=True)  16.6 us
    dot_general x1, matrix products, shards(): gate_part = jnp.dot(rows, w_gate, preferred_element_type=jnp.float32)  13.5 us
  transfers between devices with their start and end apart: 2, of which 2 were waited for; matrix products, arithmetic and copies ran while one was open for 1% of the time, Pallas kernels for 0%

profile of v1, /device:TPU:16, one launch (start us, length us, event | category | flops | bytes accessed | tf_op | source)
XLA Modules:
  0.0 213.9 jit_solution(15330885983827667369)
XLA Ops:
  6.5 0.0 all-gather.3.cloned.1.call-start
  6.5 0.7 all-gather.3.cloned.1.call-update
  7.3 0.0 reduce-scatter.2.cloned.1.call-start
  7.3 0.7 reduce_sum.18
  8.0 0.7 multiply_divide_fusion
  8.7 0.7 select_reduce_fusion
  9.4 16.6 %all-gather = f32[16,64,16]{1,2,0:T(8,128)S(1)} all-gather(f32[1,64,16]{1,2,0:T(8,128)S(1)} %bitcast.9), channel_id=1, replica_groups=mesh['group'=2,'node'=16] {'node'}, dimensions={0}, use_global_device_ids=true | all-gather | bytes 69632 | tf_op jit(solution)/shard_map/all_gather | solution.py:16
  26.1 0.1 reshape.4
  26.2 52.4 %all-gather.3.cloned.1.call-done = bf16[1024,3584]{1,0:T(8,128)(2,1)} async-done(((bf16[64,3584]{1,0:T(8,128)(2,1)}), bf16[1024,3584]{1,0:T(8,128)(2,1)}) %all-gather.3.cloned.1.call-update) | async-done | bytes 7340048 | tf_op jit(solution)/shard_map/all_gather | solution.py:19
  78.6 13.5 %fusion.2 = f32[1024,1024]{1,0:T(8,128)} fusion(bf16[1024,3584]{1,0:T(8,128)(2,1)} %all-gather.3.cloned.1.call-done, bf16[3584,1024]{1,0:T(8,128)(2,1)} %param.9), kind=kOutput, calls=%fused_computation.8 | convolution fusion | flops 7516192768 | bytes 18874368 | tf_op jit(solution)/shard_map/dot_general | solution.py:20
  92.1 24.4 %multiply_convert_fusion = bf16[1024,3584]{1,0:T(8,128)(2,1)} fusion(bf16[1024,3584]{1,0:T(8,128)(2,1)} %param.11, f32[1024]{0:T(1024)S(1)} %bitcast.10, f32[1024,1024]{1,0:T(8,128)} %fusion.2, bf16[1024,3584]{1,0:T(8,128)(2,1)} %all-gather.3.cloned.1.call-done, bf16[3584,1024]{1,0:T(8,128)(2,1)} %param.10), kind=kOutput, calls=%fused_computation | convolution fusion | flops 15046017024 | bytes 33558528 | tf_op jit(solution)/shard_map/dot_general | solution.py:23
  116.5 0.0 reduce-scatter.2.cloned.1.call-update
  116.6 90.5 %reduce-scatter.2.cloned.1.call-done = bf16[64,3584]{1,0:T(8,128)(2,1)} async-done(((bf16[1024,3584]{1,0:T(8,128)(2,1)}), bf16[64,3584]{1,0:T(8,128)(2,1)}) %reduce-scatter.2.cloned.1.call-update) | async-done | bytes 458768 | tf_op jit(solution)/shard_map/reduce_scatter | solution.py:25
  (2 shorter events, 0.1 us)
Async XLA Ops:
  6.5 72.1 %all-gather.3.cloned.1.call-start = ((), (), s32[]{:S(2)}) async-start(), calls=%async_computation.1 | async-start | bytes 7798784 | tf_op jit(solution)/shard_map/all_gather | solution.py:19
  7.3 199.9 %reduce-scatter.2.cloned.1.call-start = ((), (), s32[]{:S(2)}) async-start(), calls=%async_computation.2 | async-start | bytes 7798784 | tf_op jit(solution)/shard_map/reduce_scatter | solution.py:25
Sparse Core Ops, SparseCore 0:
  9.6 68.9 all-gather.2
  116.7 90.3 reduce-scatter.1

commit v2 on v1

v2 whole, which is shorter than its diff:
```python
import jax
import jax.numpy as jnp
from jax import lax
from jax.experimental import pallas as pl
from jax.experimental.pallas import tpu as pltpu
from jax.sharding import PartitionSpec as P

ROUTE_SCALE = 2.5
PLANES = 4
TILES = 4
LANES = 128


def routing_table(expert_ids, gate_scores, experts):
    weights = ROUTE_SCALE * gate_scores / jnp.sum(gate_scores, axis=1, keepdims=True)
    marks = expert_ids[:, :, None] == jnp.arange(experts, dtype=jnp.int32)[None, None, :]
    return jnp.sum(jnp.where(marks, weights[:, :, None], 0.0), axis=1)


def kernel(
    tok, wg_hbm, wu_hbm, wd_hbm, out,
    wg, wu, wd, rows, hidden, part, sib, ybuf, zbuf, acc,
    w_sem, gz_s, gz_r, gy_s, gy_r, gc_s, gc_r, sc_s, sc_r, sy_s, sy_r, sz_s, sz_r,
):
    n = tok.shape[0]
    features = wg_hbm.shape[0]
    hid = wg_hbm.shape[1]
    width = features // TILES
    step_cols = 256
    me = lax.axis_index("node")
    z, y, c = me // 4, (me // 2) % 2, me % 2
    top = PLANES - 1
    mine = pl.ds(pl.multiple_of(y * n, n), n)
    theirs = pl.ds(pl.multiple_of((1 - y) * n, n), n)

    def dev(zz, yy, cc):
        return {"node": zz * 4 + yy * 2 + cc}

    def remote(src, dst, s, r, target):
        return pltpu.make_async_remote_copy(
            src_ref=src, dst_ref=dst, send_sem=s, recv_sem=r,
            device_id=target, device_id_type=pl.DeviceIdType.MESH,
        )

    loads = [
        pltpu.make_async_copy(a, b, w_sem.at[i])
        for i, (a, b) in enumerate(((wg_hbm, wg), (wu_hbm, wu), (wd_hbm, wd)))
    ]
    for load in loads:
        load.start()
    rows[z, c, mine, :] = tok[...]

    barrier = pltpu.get_barrier_semaphore()

    def greet(target):
        pl.semaphore_signal(barrier, inc=1, device_id=target, device_id_type=pl.DeviceIdType.MESH)

    greet(dev(z, 1 - y, c))
    greet(dev(z, y, 1 - c))

    @pl.when(z > 0)
    def _():
        greet(dev(z - 1, y, c))

    @pl.when(z < top)
    def _():
        greet(dev(z + 1, y, c))

    pl.semaphore_wait(barrier, jnp.where(jnp.logical_or(z == 0, z == top), 3, 4))

    flip = z // 2
    m = z + flip * (top - 2 * z)

    def plane(digit):
        return digit + flip * (top - 2 * digit)

    second, third = plane(1 + m), plane(2 - 2 * m)
    last = plane(3)

    def order(k):
        return jnp.where(k == 0, z, jnp.where(k == 1, second, jnp.where(k == 2, third, last)))

    def up_copy(p):
        ref = rows.at[p, c, mine, :]
        return remote(ref, ref, gz_s.at[p, 0], gz_r.at[p], dev(z + 1, y, c))

    def down_copy(p):
        ref = rows.at[p, c, mine, :]
        return remote(ref, ref, gz_s.at[p, 1], gz_r.at[p], dev(z - 1, y, c))

    def y_copy(p):
        ref = rows.at[p, c, mine, :]
        return remote(ref, ref, gy_s.at[p], gy_r.at[p], dev(z, 1 - y, c))

    def y_arrival(p):
        ref = rows.at[p, c, theirs, :]
        return remote(ref, ref, gy_s.at[p], gy_r.at[p], dev(z, 1 - y, c))

    def core_copy(p):
        ref = rows.at[p, c]
        return remote(ref, ref, gc_s.at[p], gc_r.at[p], dev(z, y, 1 - c))

    def core_arrival(p):
        ref = rows.at[p, 1 - c]
        return remote(ref, ref, gc_s.at[p], gc_r.at[p], dev(z, y, 1 - c))

    def goes_up(p):
        return jnp.logical_and(p <= z, z < top)

    def goes_down(p):
        return jnp.logical_and(p >= z, z > 0)

    def forward(p):
        @pl.when(p != z)
        def _():
            ref = rows.at[p, c, mine, :]
            remote(ref, ref, gz_s.at[p, 0], gz_r.at[p], dev(z, 1 - y, c)).wait_recv()

        @pl.when(goes_up(p))
        def _():
            up_copy(p).start()

        @pl.when(goes_down(p))
        def _():
            down_copy(p).start()

    def advance(k):
        @pl.when(jnp.logical_and(m == 0, k <= 3))
        def _():
            forward(order(k))

        @pl.when(jnp.logical_and(m == 1, k == 1))
        def _():
            forward(second)
            forward(third)

        @pl.when(jnp.logical_and(m == 1, k == 2))
        def _():
            forward(last)

        y_copy(order(k)).start()

    def back_core(p, q):
        return remote(part.at[p, 1 - c, q], sib.at[p, q], sc_s.at[p, q], sc_r.at[p, q], dev(z, y, 1 - c))

    def back_y(p, q):
        return remote(
            part.at[p, c, q, theirs, :], ybuf.at[p, q], sy_s.at[p, q], sy_r.at[p, q], dev(z, 1 - y, c)
        )

    def back_z(p, q):
        up = p > z
        slot = jnp.where(p == z + 1, PLANES, p)
        return remote(
            part.at[p, c, q, mine, :], zbuf.at[slot, q], sz_s.at[p, q], sz_r.at[slot, q],
            dev(jnp.where(up, z + 1, z - 1), y, c),
        )

    def z_arrival(slot, q):
        ref = zbuf.at[slot, q]
        return remote(ref, ref, sz_s.at[0, q], sz_r.at[slot, q], dev(z, 1 - y, c))

    def down_project(p, q, share):
        cols = pl.ds(pl.multiple_of(q * width, width), width)
        piece = jnp.dot(hidden[...], wd[:, cols], preferred_element_type=jnp.float32)
        piece = (piece * share).astype(jnp.bfloat16)
        part[p, 0, q] = piece[: 2 * n]
        part[p, 1, q] = piece[2 * n :]
        back_core(p, q).start()

    def add_core(p, q):
        back_core(p, q).wait_recv()
        total = part[p, c, q].astype(jnp.float32) + sib[p, q].astype(jnp.float32)
        part[p, c, q] = total.astype(jnp.bfloat16)
        back_y(p, q).start()

    def add_rest(p):
        def body(q, _):
            back_y(p, q).wait_recv()
            acc[...] = part[p, c, q, mine, :].astype(jnp.float32) + ybuf[p, q].astype(jnp.float32)

            def take(slot):
                z_arrival(slot, q).wait_recv()
                acc[...] += zbuf[slot, q].astype(jnp.float32)

            @pl.when(jnp.logical_or(jnp.logical_and(p > z, z > 0), jnp.logical_and(p <= z, z < top)))
            def _():
                take(p)

            @pl.when(jnp.logical_and(p == z, z > 0))
            def _():
                take(PLANES)

            @pl.when(p == z)
            def _():
                out[:, pl.ds(pl.multiple_of(q * width, width), width)] = acc[...].astype(jnp.bfloat16)

            @pl.when(p != z)
            def _():
                part[p, c, q, mine, :] = acc[...].astype(jnp.bfloat16)
                back_z(p, q).start()

            return 0

        lax.fori_loop(0, TILES, body, 0)

    forward(z)
    y_copy(z).start()

    def stage(k, _):
        p = order(k)
        y_arrival(p).wait_recv()
        core_copy(p).start()

        @pl.when(k < top)
        def _():
            advance(k + 1)

        @pl.when(jnp.logical_and(m == 0, k >= 2))
        def _():
            add_rest(order(k - 1))

        core_arrival(p).wait_recv()

        @pl.when(k == 0)
        def _():
            loads[0].wait()
            loads[1].wait()

        table = rows[p, :, :, features:].reshape(4 * n, LANES).astype(jnp.float32)
        lane = lax.broadcasted_iota(jnp.int32, (4 * n, LANES), 1)
        chosen = jnp.logical_or(lane == me, lane == me + LANES // 2)
        share = jnp.sum(jnp.where(chosen, table, 0.0), axis=1, keepdims=True)

        def up_project(j, _):
            cols = pl.ds(pl.multiple_of(j * step_cols, step_cols), step_cols)
            x = rows[p, :, :, :features].reshape(4 * n, features)
            gate = jnp.dot(x, wg[:, cols], preferred_element_type=jnp.float32)
            up = jnp.dot(x, wu[:, cols], preferred_element_type=jnp.float32)
            hidden[:, cols] = (gate / (1.0 + jnp.exp(-gate)) * up).astype(jnp.bfloat16)
            return 0

        lax.fori_loop(0, hid // step_cols, up_project, 0)

        @pl.when(k == 0)
        def _():
            loads[2].wait()

        def down(q, _):
            down_project(p, q, share)

            @pl.when(q > 0)
            def _():
                add_core(p, q - 1)

            return 0

        lax.fori_loop(0, TILES, down, 0)
        add_core(p, TILES - 1)
        return 0

    lax.fori_loop(0, PLANES, stage, 0)

    add_rest(last)

    @pl.when(m == 1)
    def _():
        add_rest(third)
        add_rest(second)

    add_rest(z)

    def settle(p, _):
        @pl.when(goes_up(p))
        def _():
            up_copy(p).wait_send()

        @pl.when(goes_down(p))
        def _():
            down_copy(p).wait_send()

        y_copy(p).wait_send()
        core_copy(p).wait_send()

        def tiles(q, _):
            back_core(p, q).wait_send()
            back_y(p, q).wait_send()

            @pl.when(p != z)
            def _():
                back_z(p, q).wait_send()

            return 0

        lax.fori_loop(0, TILES, tiles, 0)
        return 0

    lax.fori_loop(0, PLANES, settle, 0)


def meshed(tokens, expert_ids, gate_scores, w_gate, w_up, w_down):
    n, features = tokens.shape
    hid = w_gate.shape[1]
    width = features // TILES
    experts = lax.axis_size("node")
    table = routing_table(expert_ids, gate_scores, experts)
    high = table.astype(jnp.bfloat16)
    low = (table - high.astype(jnp.float32)).astype(jnp.bfloat16)
    gap = jnp.zeros((n, LANES // 2 - experts), jnp.bfloat16)
    tok = jnp.concatenate([tokens, high, gap, low, gap], axis=1)
    bf = jnp.bfloat16
    dma = pltpu.SemaphoreType.DMA
    return pl.pallas_call(
        kernel,
        out_shape=jax.ShapeDtypeStruct((n, features), bf),
        in_specs=[pl.BlockSpec(memory_space=pltpu.VMEM)] + [pl.BlockSpec(memory_space=pl.ANY)] * 3,
        out_specs=pl.BlockSpec(memory_space=pltpu.VMEM),
        scratch_shapes=[
            pltpu.VMEM((features, hid), bf),
            pltpu.VMEM((features, hid), bf),
            pltpu.VMEM((hid, features), bf),
            pltpu.VMEM((PLANES, 2, 2 * n, features + LANES), bf),
            pltpu.VMEM((4 * n, hid), bf),
            pltpu.VMEM((PLANES, 2, TILES, 2 * n, width), bf),
            pltpu.VMEM((PLANES, TILES, 2 * n, width), bf),
            pltpu.VMEM((PLANES, TILES, n, width), bf),
            pltpu.VMEM((PLANES + 1, TILES, n, width), bf),
            pltpu.VMEM((n, width), jnp.float32),
            dma((3,)),
            dma((PLANES, 2)), dma((PLANES,)),
            dma((PLANES,)), dma((PLANES,)),
            dma((PLANES,)), dma((PLANES,)),
            dma((PLANES, TILES)), dma((PLANES, TILES)),
            dma((PLANES, TILES)), dma((PLANES, TILES)),
            dma((PLANES, TILES)), dma((PLANES + 1, TILES)),
        ],
        compiler_params=pltpu.CompilerParams(
            collective_id=0, has_side_effects=True, vmem_limit_bytes=62 * 1024 * 1024
        ),
        cost_estimate=pl.CostEstimate(
            flops=6 * 16 * n * features * hid, bytes_accessed=6 * features * hid, transcendentals=16 * n * hid
        ),
    )(tok, w_gate, w_up, w_down)


def gathered(tokens, expert_ids, gate_scores, w_gate, w_up, w_down):
    node_count = lax.axis_size("node")
    experts = max(16, node_count // 2)
    slices = node_count // experts
    table = routing_table(expert_ids, gate_scores, experts)
    all_table = lax.all_gather(table, "node", axis=0, tiled=True)
    share = lax.dynamic_slice_in_dim(all_table, lax.axis_index("node") // slices, 1, 1)
    rows = lax.all_gather(tokens, "node", axis=0, tiled=True)
    gate_part = jnp.dot(rows, w_gate, preferred_element_type=jnp.float32)
    up_part = jnp.dot(rows, w_up, preferred_element_type=jnp.float32)
    hidden = (jax.nn.silu(gate_part) * up_part).astype(jnp.bfloat16)
    piece = jnp.dot(hidden, w_down, preferred_element_type=jnp.float32)
    part = piece * share
    return lax.psum_scatter(part, "node", scatter_dimension=0, tiled=True).astype(jnp.bfloat16)


def solution(mesh):
    return jax.shard_map(
        meshed if mesh.shape["node"] == 16 else gathered,
        mesh=mesh,
        in_specs=(
            P(("group", "node"), None),
            P(("group", "node"), None),
            P(("group", "node"), None),
            P(None, "node"),
            P(None, "node"),
            P("node", None),
        ),
        out_specs=P(("group", "node"), None),
        check_vma=False,
    )
```

time: 216 us -> 123 us (0.57)
  waiting for transfers between devices: 144 us -> 0 us
  Pallas kernels: 0 us -> 117 us
  matrix products: 37.9 us -> 0 us
  blocking collectives: 16.6 us -> 0 us
  between operations: 13.4 us -> 0.03 us
  local copies, waits for them, and re-layouts: 0.15 us -> 3.88 us
    pallas_call x0 -> x1, Pallas kernels: none -> 117 us  [meshed(): pl.pallas_call(kernel, out_shape=jax.ShapeDtypeStruct((n, features), bf),...]
    reduce_scatter x1 -> x0, waiting for transfers between devices: 90.5 us -> none  [shards(): return lax.psum_scatter(part, 'node', scatter_dimension=0, tiled=True)]
    all_gather x1 -> x0, waiting for transfers between devices: 52.4 us -> none  [shards(): rows = lax.all_gather(tokens, 'node', axis=0, tiled=True)]
    dot_general x2 -> x0, matrix products: 37.9 us -> none  [the longest x1 24.4 us: shards(): piece = jnp.dot(hidden, w_down, preferred_element_type=jnp.float32)]
    all_gather x1 -> x0, blocking collectives: 16.6 us -> none  [shards(): all_table = lax.all_gather(table, 'node', axis=0, tiled=True)]
  transfers between devices with their start and end apart: 2 -> 0, of which waited for: 2 -> 0; matrix products, arithmetic and copies ran while one was open for 1% -> 0% of each run, Pallas kernels for 0% -> 0%
where the time goes in v2:
time: 123 us
  Pallas kernels  117 us (95%)
  local copies, waits for them, and re-layouts  3.88 us (3%)
  other arithmetic  2.11 us (2%)
    pallas_call x1, Pallas kernels, meshed(): pl.pallas_call(kernel, out_shape=jax.ShapeDtypeStruct((n, features), bf),...  117 us

profile of v2, /device:TPU:16, one launch (start us, length us, event | category | flops | bytes accessed | tf_op | source)
XLA Modules:
  0.0 122.8 jit_solution(11932410642312110217)
XLA Ops:
  0.0 0.7 reduce_sum.18
  0.7 0.7 multiply_divide_fusion
  1.4 0.7 select_reduce_fusion
  2.1 0.1 copy.13
  2.2 0.1 copy.12
  2.3 1.9 %concatenate.3.tok = bf16[64,3712]{1,0:T(8,128)(2,1)} concatenate(bf16[64,3584]{1,0:T(8,128)(2,1)} %param.6, bf16[64,16]{1,0:T(8,128)(2,1)S(1)} %copy.13, bf16[64,48]{1,0:T(8,128)(2,1)S(1)} %broadcast_in_dim.21, bf16[64,16]{1,0:T(8,128)(2,1)S(1)} %subtract_convert_fusion, bf16[64,48]{1,0:T(8,128)(2,1)S(1)} %broadcast_in_dim.21), dimensions={1} | concatenate | bytes 950272 | tf_op jit(solution)/shard_map/concatenate | solution.py:310
  4.2 116.8 %shard_map.64 = bf16[64,3584]{1,0:T(8,128)(2,1)} custom-call(bf16[64,3712]{1,0:T(8,128)(2,1)} %concatenate.3.tok, bf16[3584,1024]{1,0:T(8,128)(2,1)} %wg_hbm.1, bf16[3584,1024]{1,0:T(8,128)(2,1)} %wu_hbm.1, bf16[1024,3584]{1,0:T(8,128)(2,1)} %wd_hbm.1), custom_call_target="tpu_custom_call" | custom-call | flops 22548578304 | bytes 22020096 | tf_op jit(solution)/shard_map/pallas_call | solution.py:313
  121.0 1.8 %copy.15 = bf16[64,3584]{1,0:T(8,128)(2,1)} copy(bf16[64,3584]{1,0:T(8,128)(2,1)} %shard_map.64) | data formatting | bytes 917504
  (3 shorter events, 0.0 us)

commit v3 on v2

--- a/solution.py
+++ b/solution.py
@@ -9,6 +9,7 @@
 PLANES = 4
 TILES = 4
 LANES = 128
+FAR = 1
 
 
 def routing_table(expert_ids, gate_scores, experts):
@@ -20,7 +21,7 @@
 def kernel(
     tok, wg_hbm, wu_hbm, wd_hbm, out,
     wg, wu, wd, rows, hidden, part, sib, ybuf, zbuf, acc,
-    w_sem, gz_s, gz_r, gy_s, gy_r, gc_s, gc_r, sc_s, sc_r, sy_s, sy_r, sz_s, sz_r,
+    w_sem, gz_s, gz_r, gy_s, gy_r, gb_s, gb_r, gc_s, gc_r, sc_s, sc_r, sy_s, sy_r, sz_s, sz_r,
 ):
     n = tok.shape[0]
     features = wg_hbm.shape[0]
@@ -32,6 +33,13 @@
     top = PLANES - 1
     mine = pl.ds(pl.multiple_of(y * n, n), n)
     theirs = pl.ds(pl.multiple_of((1 - y) * n, n), n)
+    tail = n // 4
+
+    def part_rows(which):
+        if which == 0:
+            return pl.ds(pl.multiple_of(y * n, n), n - tail)
+        at = y if which == 1 else 1 - y
+        return pl.ds(pl.multiple_of(at * n + n - tail, tail), tail)
 
     def dev(zz, yy, cc):
         return {"node": zz * 4 + yy * 2 + cc}
@@ -80,21 +88,24 @@
     def order(k):
         return jnp.where(k == 0, z, jnp.where(k == 1, second, jnp.where(k == 2, third, last)))
 
-    def up_copy(p):
-        ref = rows.at[p, c, mine, :]
-        return remote(ref, ref, gz_s.at[p, 0], gz_r.at[p], dev(z + 1, y, c))
-
-    def down_copy(p):
-        ref = rows.at[p, c, mine, :]
-        return remote(ref, ref, gz_s.at[p, 1], gz_r.at[p], dev(z - 1, y, c))
+    def z_copy(p, which, up):
+        ref = rows.at[p, c, part_rows(which), :]
+        way = 0 if up else 1
+        return remote(
+            ref, ref, gz_s.at[p, way, which], gz_r.at[p, which], dev(z + 1 if up else z - 1, y, c)
+        )
 
     def y_copy(p):
-        ref = rows.at[p, c, mine, :]
+        ref = rows.at[p, c, part_rows(0), :]
         return remote(ref, ref, gy_s.at[p], gy_r.at[p], dev(z, 1 - y, c))
 
     def y_arrival(p):
-        ref = rows.at[p, c, theirs, :]
+        ref = rows.at[p, c, pl.ds(pl.multiple_of((1 - y) * n, n), n - tail), :]
         return remote(ref, ref, gy_s.at[p], gy_r.at[p], dev(z, 1 - y, c))
+
+    def tail_copy(which):
+        ref = rows.at[z, c, part_rows(which), :]
+        return remote(ref, ref, gb_s.at[0], gb_r.at[0], dev(z, 1 - y, c))
 
     def core_copy(p):
         ref = rows.at[p, c]
@@ -110,33 +121,37 @@
     def goes_down(p):
         return jnp.logical_and(p >= z, z > 0)
 
-    def forward(p):
+    def forward(p, which):
         @pl.when(p != z)
         def _():
-            ref = rows.at[p, c, mine, :]
-            remote(ref, ref, gz_s.at[p, 0], gz_r.at[p], dev(z, 1 - y, c)).wait_recv()
+            ref = rows.at[p, c, part_rows(which), :]
+            remote(ref, ref, gz_s.at[p, 0, which], gz_r.at[p, which], dev(z, 1 - y, c)).wait_recv()
 
         @pl.when(goes_up(p))
         def _():
-            up_copy(p).start()
+            z_copy(p, which, True).start()
 
         @pl.when(goes_down(p))
         def _():
-            down_copy(p).start()
+            z_copy(p, which, False).start()
+
+    def forward_all(p):
+        for which in range(3):
+            forward(p, which)
 
     def advance(k):
         @pl.when(jnp.logical_and(m == 0, k <= 3))
         def _():
-            forward(order(k))
+            forward_all(order(k))
 
         @pl.when(jnp.logical_and(m == 1, k == 1))
         def _():
-            forward(second)
-            forward(third)
+            forward_all(second)
+            forward_all(third)
 
         @pl.when(jnp.logical_and(m == 1, k == 2))
         def _():
-            forward(last)
+            forward_all(last)
 
         y_copy(order(k)).start()
 
@@ -151,13 +166,16 @@
     def back_z(p, q):
         up = p > z
         slot = jnp.where(p == z + 1, PLANES, p)
+        target = dev(jnp.where(up, z + 1, z - 1), y, c)
+        if q < FAR:
+            return remote(part.at[p, c, q], zbuf.at[slot, q], sz_s.at[p, q], sz_r.at[slot, q], target)
         return remote(
-            part.at[p, c, q, mine, :], zbuf.at[slot, q], sz_s.at[p, q], sz_r.at[slot, q],
-            dev(jnp.where(up, z + 1, z - 1), y, c),
+            part.at[p, c, q, mine, :], zbuf.at[slot, q, pl.ds(0, n), :],
+            sz_s.at[p, q], sz_r.at[slot, q], target,
         )
 
     def z_arrival(slot, q):
-        ref = zbuf.at[slot, q]
+        ref = zbuf.at[slot, q] if q < FAR else zbuf.at[slot, q, pl.ds(0, n), :]
         return remote(ref, ref, sz_s.at[0, q], sz_r.at[slot, q], dev(z, 1 - y, c))
 
     def down_project(p, q, share):
@@ -172,16 +190,26 @@
         back_core(p, q).wait_recv()
         total = part[p, c, q].astype(jnp.float32) + sib[p, q].astype(jnp.float32)
         part[p, c, q] = total.astype(jnp.bfloat16)
-        back_y(p, q).start()
+
+        @pl.when(q >= FAR)
+        def _():
+            back_y(p, q).start()
 
     def add_rest(p):
-        def body(q, _):
-            back_y(p, q).wait_recv()
-            acc[...] = part[p, c, q, mine, :].astype(jnp.float32) + ybuf[p, q].astype(jnp.float32)
-
-            def take(slot):
+        for q in range(TILES):
+            far = q < FAR
+            span = 2 * n if far else n
+            here = part.at[p, c, q] if far else part.at[p, c, q, mine, :]
+            total = acc.at[pl.ds(0, span), :]
+            if far:
+                total[...] = here[...].astype(jnp.float32)
+            else:
+                back_y(p, q).wait_recv()
+                total[...] = here[...].astype(jnp.float32) + ybuf[p, q].astype(jnp.float32)
+
+            def take(slot, q=q, span=span, total=total):
                 z_arrival(slot, q).wait_recv()
-                acc[...] += zbuf[slot, q].astype(jnp.float32)
+                total[...] += zbuf[slot, q, pl.ds(0, span), :].astype(jnp.float32)
 
             @pl.when(jnp.logical_or(jnp.logical_and(p > z, z > 0), jnp.logical_and(p <= z, z < top)))
             def _():
@@ -191,21 +219,31 @@
             def _():
                 take(PLANES)
 
-            @pl.when(p == z)
-            def _():
-                out[:, pl.ds(pl.multiple_of(q * width, width), width)] = acc[...].astype(jnp.bfloat16)
+            if far:
+                here[...] = total[...].astype(jnp.bfloat16)
+
+                @pl.when(p == z)
+                def _():
+                    back_y(p, q).start()
+            else:
+                @pl.when(p == z)
+                def _():
+                    out[:, q * width : (q + 1) * width] = total[...].astype(jnp.bfloat16)
+
+                @pl.when(p != z)
+                def _():
+                    here[...] = total[...].astype(jnp.bfloat16)
 
             @pl.when(p != z)
             def _():
-                part[p, c, q, mine, :] = acc[...].astype(jnp.bfloat16)
                 back_z(p, q).start()
 
-            return 0
-
-        lax.fori_loop(0, TILES, body, 0)
-
-    forward(z)
+    tail_copy(1).start()
+    forward(z, 0)
+    forward(z, 1)
     y_copy(z).start()
+    tail_copy(2).wait_recv()
+    forward(z, 2)
 
     def stage(k, _):
         p = order(k)
@@ -261,41 +299,48 @@
 
     lax.fori_loop(0, PLANES, stage, 0)
 
-    add_rest(last)
-
-    @pl.when(m == 1)
-    def _():
-        add_rest(third)
-        add_rest(second)
-
-    add_rest(z)
+    def remaining(i, _):
+        @pl.when(jnp.logical_or(m == 1, jnp.logical_or(i == 1, i == 3)))
+        def _():
+            add_rest(jnp.where(i == 0, second, jnp.where(i == 1, last, jnp.where(i == 2, third, z))))
+
+        return 0
+
+    lax.fori_loop(0, PLANES, remaining, 0)
+    for q in range(FAR):
+        back_y(z, q).wait_recv()
+        total = part[z, c, q, mine, :].astype(jnp.float32) + ybuf[z, q].astype(jnp.float32)
+        out[:, q * width : (q + 1) * width] = total.astype(jnp.bfloat16)
 
     def settle(p, _):
         @pl.when(goes_up(p))
         def _():
-            up_copy(p).wait_send()
+            for which in range(3):
+                z_copy(p, which, True).wait_send()
 
         @pl.when(goes_down(p))
         def _():
-            down_copy(p).wait_send()
+            for which in range(3):
+                z_copy(p, which, False).wait_send()
 
         y_copy(p).wait_send()
         core_copy(p).wait_send()
 
-        def tiles(q, _):
+        for q in range(TILES):
             back_core(p, q).wait_send()
-            back_y(p, q).wait_send()
+
+            @pl.when(jnp.logical_or(q >= FAR, p == z))
+            def _():
+                back_y(p, q).wait_send()
 
             @pl.when(p != z)
             def _():
                 back_z(p, q).wait_send()
 
-            return 0
-
-        lax.fori_loop(0, TILES, tiles, 0)
         return 0
 
     lax.fori_loop(0, PLANES, settle, 0)
+    tail_copy(1).wait_send()
 
 
 def meshed(tokens, expert_ids, gate_scores, w_gate, w_up, w_down):
@@ -324,11 +369,12 @@
             pltpu.VMEM((PLANES, 2, TILES, 2 * n, width), bf),
             pltpu.VMEM((PLANES, TILES, 2 * n, width), bf),
             pltpu.VMEM((PLANES, TILES, n, width), bf),
-            pltpu.VMEM((PLANES + 1, TILES, n, width), bf),
-            pltpu.VMEM((n, width), jnp.float32),
+            pltpu.VMEM((PLANES + 1, TILES, 2 * n, width), bf),
+            pltpu.VMEM((2 * n, width), jnp.float32),
             dma((3,)),
-            dma((PLANES, 2)), dma((PLANES,)),
+            dma((PLANES, 2, 3)), dma((PLANES, 3)),
             dma((PLANES,)), dma((PLANES,)),
+            dma((1,)), dma((1,)),
             dma((PLANES,)), dma((PLANES,)),
             dma((PLANES, TILES)), dma((PLANES, TILES)),
             dma((PLANES, TILES)), dma((PLANES, TILES)),

time: 123 us -> 115 us (0.935)
  the two profiles are of different devices: /device:TPU:16 before, /device:TPU:0 now
where the time goes in v3:
time: 115 us
  Pallas kernels  109 us (95%)
  local copies, waits for them, and re-layouts  3.88 us (3%)
  other arithmetic  2.11 us (2%)
    pallas_call x1, Pallas kernels, meshed(): pl.pallas_call(kernel, out_shape=jax.ShapeDtypeStruct((n, features), bf),...  109 us

profile of v3, /device:TPU:0, one launch (start us, length us, event | category | flops | bytes accessed | tf_op | source)
XLA Modules:
  0.0 115.0 jit_solution(6906572664055707229)
XLA Ops:
  0.0 0.7 reduce_sum.18
  0.7 0.7 multiply_divide_fusion
  1.4 0.7 select_reduce_fusion
  2.1 0.1 copy.13
  2.2 0.1 copy.12
  2.3 1.9 %concatenate.3.tok = bf16[64,3712]{1,0:T(8,128)(2,1)} concatenate(bf16[64,3584]{1,0:T(8,128)(2,1)} %param.6, bf16[64,16]{1,0:T(8,128)(2,1)S(1)} %copy.13, bf16[64,48]{1,0:T(8,128)(2,1)S(1)} %broadcast_in_dim.21, bf16[64,16]{1,0:T(8,128)(2,1)S(1)} %subtract_convert_fusion, bf16[64,48]{1,0:T(8,128)(2,1)S(1)} %broadcast_in_dim.21), dimensions={1} | concatenate | bytes 950272 | tf_op jit(solution)/shard_map/concatenate | solution.py:355
  4.2 109.0 %shard_map.64 = bf16[64,3584]{1,0:T(8,128)(2,1)} custom-call(bf16[64,3712]{1,0:T(8,128)(2,1)} %concatenate.3.tok, bf16[3584,1024]{1,0:T(8,128)(2,1)} %wg_hbm.1, bf16[3584,1024]{1,0:T(8,128)(2,1)} %wu_hbm.1, bf16[1024,3584]{1,0:T(8,128)(2,1)} %wd_hbm.1), custom_call_target="tpu_custom_call" | custom-call | flops 22548578304 | bytes 22020096 | tf_op jit(solution)/shard_map/pallas_call | solution.py:358
  113.2 1.8 %copy.15 = bf16[64,3584]{1,0:T(8,128)(2,1)} copy(bf16[64,3584]{1,0:T(8,128)(2,1)} %shard_map.64) | data formatting | bytes 917504
  (3 shorter events, 0.0 us)
